TPU v7x, 512 devices: a whole 4x8x8 slice. The times are simulated.
512 devices in a mesh: space: 64 (over y_lo, z, core), samp: 8 (over x, y_hi).
Axes of the slice: x: 4, y: 8 (y_hi: 2, y_lo: 4; y = y_hi * 4 + y_lo), z: 8, core: 2. Of those that a mesh axis runs over, the one named last changes fastest.
Arguments:
- snapshots: float32 [4, 512, 131072], P(None, 'samp', 'space'), may hold values from -24 to 24
- space_basis: float32 [256, 131072], P('samp', 'space'), may hold values from -0.016572815 to 0.016572815
- sample_basis: float32 [512, 64], P('samp'), may hold values from -0.26516504 to 0.26516504
Outputs:
- deflated: float32 [4, 512, 131072], P(None, 'samp', 'space')
All inputs are finite; a program needn't handle non-finite values.
Results may differ from a plain program's by a relative error of at most 0.000078.
Values sent between devices are 32-bit elements; how exact they have to be, the bound alone decides.
A program may use at most 64 MiB of HBM per device.

v0:
```python
import jax
import jax.numpy as jnp
from jax import lax
from jax.sharding import PartitionSpec as P


def copy_for_each(shard, axis):
    copies = jnp.broadcast_to(shard, (lax.axis_size(axis), *shard.shape))
    return lax.all_to_all(copies, axis, split_axis=0, concat_axis=0, tiled=True)


def in_order(tiles, dim):
    tiles = jnp.moveaxis(tiles, 0, dim)
    shape = tiles.shape
    return tiles.reshape(*shape[:dim], shape[dim] * shape[dim + 1], *shape[dim + 2 :])


def gather_directly(shard, axis, dim):
    tiles = copy_for_each(shard, axis)
    return in_order(tiles, dim)


def cut_along(shard, dim, length):
    before, after = (shard.shape[:dim], shard.shape[dim + 1 :])
    return jnp.moveaxis(shard.reshape(*before, length, -1, *after), dim, 0)


def sum_at_owner(shard, axis, dim):
    tiles = cut_along(shard, dim, lax.axis_size(axis))
    arrived = lax.all_to_all(tiles, axis, split_axis=0, concat_axis=0, tiled=True)
    return arrived.sum(axis=0)


def over_copies(shard, axis):
    return copy_for_each(shard, axis).sum(axis=0)


def shards(snapshots, space_basis, sample_basis):
    highest = lax.Precision.HIGHEST
    snap_count, local_samples, row_count = snapshots.shape
    rank_samples = sample_basis.shape[1]
    full_basis = gather_directly(space_basis, "samp", 0)
    rank_rows = full_basis.shape[0]
    flattened = snapshots.reshape(snap_count * local_samples, row_count)
    row_terms = sum_at_owner(
        lax.dot_general(
            full_basis,
            flattened,
            (((1,), (1,)), ((), ())),
            precision=highest,
            preferred_element_type=jnp.float32,
        ),
        "space",
        0,
    )
    shaped = row_terms.reshape(row_terms.shape[0], snap_count, local_samples)
    result = jnp.einsum("rts,sq->rtq", shaped, sample_basis, precision=highest)
    core_rows = over_copies(result.reshape(row_terms.shape[0], snap_count * rank_samples), "samp")
    core_full = gather_directly(core_rows, "space", 0)
    core_shaped = core_full.reshape(rank_rows, snap_count, rank_samples)
    spread = jnp.einsum("rtq,sq->rts", core_shaped, sample_basis, precision=highest)
    spread = spread.reshape(rank_rows, snap_count * local_samples)
    removed = lax.dot_general(
        spread,
        full_basis,
        (((0,), (0,)), ((), ())),
        precision=highest,
        preferred_element_type=jnp.float32,
    )
    return snapshots - removed.reshape(snap_count, local_samples, row_count)


def solution(mesh):
    return jax.shard_map(
        shards,
        mesh=mesh,
        in_specs=(P(None, "samp", "space"), P("samp", "space"), P("samp", None)),
        out_specs=P(None, "samp", "space"),
        check_vma=False,
    )
```

profile of v0, /device:TPU:1, one launch (start us, length us, event | category | flops | bytes accessed | tf_op | source)
XLA Modules:
  0.0 131.1 jit_solution(9572793325473403727)
XLA Ops:
  0.0 0.0 copy-start
  0.0 1.2 broadcast_in_dim.9
  1.2 51.8 %all_to_all.20 = f32[8,32,2048]{2,1,0:T(8,128)S(1)} all-to-all(f32[8,32,2048]{2,1,0:T(8,128)S(1)} %broadcast_in_dim.9), channel_id=1, replica_groups=mesh['space'=64,'samp'=8] {'samp'}, dimensions={0} | all-to-all | bytes 4194304 | tf_op jit(solution)/shard_map/all_to_all | solution.py:9
  53.0 1.6 %dot_general.18 = f32[64,4,2048]{2,1,0:T(4,128)} reshape(f32[8,32,2048]{2,1,0:T(8,128)S(1)} %all_to_all.20) | data formatting | bytes 4194304 | tf_op jit(solution)/shard_map/dot_general | solution.py:46
  54.6 5.1 %fusion = f32[64,4,256]{2,0,1:T(8,128)S(1)} fusion(f32[256,2048,1]{1,0,2:T(8,128)} %bitcast.22, f32[64,4,2048]{2,1,0:T(4,128)} %dot_general.18), kind=kOutput, calls=%fused_computation.1 | convolution fusion | flops 1610612736 | bytes 4456448 | tf_op jit(solution)/shard_map/dot_general | solution.py:46
  59.7 0.2 copy.13
  59.9 34.8 %all_to_all.21 = f32[64,4,256]{2,1,0:T(4,128)S(1)} all-to-all(f32[64,4,256]{2,1,0:T(4,128)S(1)} %copy.13), channel_id=1, replica_groups=mesh['space'=64,'samp'=8] {'space'}, dimensions={0} | all-to-all | bytes 524288 | tf_op jit(solution)/shard_map/all_to_all | solution.py:30
  94.7 0.1 reduce_sum.18
  94.8 0.1 reshape.21
  94.9 0.0 copy-done
  94.9 0.2 fusion.4
  95.1 0.1 reshape.22
  95.2 11.4 %all_to_all.22 = f32[8,4,256]{2,1,0:T(4,128)S(1)} all-to-all(f32[8,4,256]{2,1,0:T(4,128)S(1)} %broadcast_in_dim.10), channel_id=1, replica_groups=mesh['space'=64,'samp'=8] {'samp'}, dimensions={0} | all-to-all | bytes 65536 | tf_op jit(solution)/shard_map/all_to_all | solution.py:9
  106.6 18.7 %all_to_all.23 = f32[64,4,256]{2,1,0:T(4,128)S(1)} all-to-all(f32[64,4,256]{2,1,0:T(4,128)S(1)} %broadcast_in_dim.11), channel_id=1, replica_groups=mesh['space'=64,'samp'=8] {'space'}, dimensions={0} | all-to-all | bytes 524288 | tf_op jit(solution)/shard_map/all_to_all | solution.py:9
  125.3 0.3 reshape_reshape.3
  125.6 0.7 convolution_bitcast_fusion
  126.3 4.8 %convolution_subtract_fusion = f32[4,64,2048]{2,1,0:T(8,128)} fusion(f32[4,64,2048]{2,1,0:T(8,128)} %param.3, f32[4,64,256]{2,1,0:T(8,128)S(1)} %convolution_bitcast_fusion, f32[256,2048,1]{1,0,2:T(8,128)S(1)} %bitcast.21), kind=kOutput, calls=%fused_computation | convolution fusion | flops 1611137024 | bytes 6553600 | tf_op jit(solution)/shard_map/dot_general | solution.py:63
  (3 shorter events, 0.1 us)
Async XLA Ops:
  0.0 94.9 %copy-start = (f32[64,64]{1,0:T(8,128)S(1)}, f32[64,64]{1,0:T(8,128)}, u32[]{:S(2)}) copy-start(f32[64,64]{1,0:T(8,128)} %param.5) | copy-start | bytes 49156
where the time goes:
time: 131 us
  blocking collectives  117 us (89%)
  matrix products  10.8 us (8%)
  local copies, waits for them, and re-layouts  3.5 us (3%)
    all_to_all x3, blocking collectives, copy_for_each(): return lax.all_to_all(copies, axis, split_axis=0, concat_axis=0, tiled=True)  81.8 us
    all_to_all x1, blocking collectives, sum_at_owner(): lax.all_to_all(tiles, axis, split_axis=0, concat_axis=0, tiled=True)  34.8 us
    dot_general x1, matrix products, shards(): lax.dot_general(full_basis, flattened, (((1,), (1,)), ((), ())), precisio...  5.11 us
    dot_general x1, matrix products, shards(): lax.dot_general(spread, full_basis, (((0,), (0,)), ((), ())), precision=h...  4.83 us

commit v1 on v0

v1 whole, which is shorter than its diff:
```python
import jax
import jax.numpy as jnp
from jax import lax
from jax.experimental import pallas as pl
from jax.experimental.pallas import tpu as pltpu
from jax.sharding import PartitionSpec as P

MESH = pl.DeviceIdType.MESH
f32, bf16 = jnp.float32, jnp.bfloat16
XS, YS, ZS, CORES = 4, 8, 8, 2
CHUNKS = 4
TILE = 256


def position():
    space, samp = lax.axis_index("space"), lax.axis_index("samp")
    core, z = lax.rem(space, 2), lax.rem(space // 2, 8)
    y_lo, y_hi = space // 16, lax.rem(samp, 2)
    return samp // 2, y_hi * 4 + y_lo, z, core


def device(at, dx=0, dy=0, dz=0, dc=0):
    x, y, z, core = at
    x, y, z = lax.rem(x + dx, XS), lax.rem(y + dy, YS), lax.rem(z + dz, ZS)
    core = lax.rem(core + dc, CORES)
    return {
        "space": (lax.rem(y, 4) * ZS + z) * 2 + core,
        "samp": x * 2 + y // 4,
    }


NEAR = [(dx, dc) for dx in range(XS) for dc in range(CORES) if (dx, dc) != (0, 0)]


def halves(value):
    high = value.astype(bf16)
    return high, (value - high.astype(f32)).astype(bf16)


def nn(a, b):
    return jnp.dot(a, b, preferred_element_type=f32)


def nt(a, b):
    return lax.dot_general(a, b, (((1,), (1,)), ((), ())), preferred_element_type=f32)


def kernel(
    x_hbm, b_hbm, a_hbm, out_v,
    x_v, a_v, basis, bhi, blo, yhi, ylo, diag, dhi, dlo, thi, tlo,
    part, rs_in, rs_sum, z_in, z_sum, y_in, core, shi, slo,
    load_sem, sy, ry, sx, rx, sxf, rxf, sp, rp, spf, rpf,
    s_rs, r_rs, s_z, r_z, s_y, r_y, s_ag, r_ag,
):
    at = position()
    x, y, z, c = at
    mine = y // 4
    other = 1 - mine

    loads = [
        pltpu.make_async_copy(b_hbm, basis.at[mine, x], load_sem.at[0]),
        pltpu.make_async_copy(a_hbm, a_v, load_sem.at[1]),
        pltpu.make_async_copy(x_hbm, x_v, load_sem.at[2]),
    ]
    for load in loads:
        load.start()

    barrier = pltpu.get_barrier_semaphore()
    partners = [dict(dx=dx, dc=dc) for dx, dc in NEAR]
    partners += [dict(dz=d) for d in range(1, ZS)] + [dict(dy=d) for d in range(1, YS)]
    for partner in partners:
        pl.semaphore_signal(
            barrier, inc=1, device_id=device(at, **partner), device_id_type=MESH
        )
    diag[...] = jnp.zeros_like(diag)
    pl.semaphore_wait(barrier, len(partners))

    started = []

    def remote(src, dst, send, recv, **offset):
        return pltpu.make_async_remote_copy(
            src_ref=src,
            dst_ref=dst,
            send_sem=send,
            recv_sem=recv,
            device_id=device(at, **offset),
            device_id_type=MESH,
        )

    def go(copy):
        copy.start()
        started.append(copy)

    step = (1, XS - 1)

    def own_rows(d, half, block_x):
        ref = basis.at[mine, block_x, pl.ds(half * 16, 16)]
        return remote(ref, ref, sx.at[d, half], rx.at[d, half], dx=step[d])

    def own_forward(d, block_x):
        ref = basis.at[mine, block_x, pl.ds(d * 16, 16)]
        return remote(ref, ref, sxf.at[d], rxf.at[d], dx=step[d])

    def across(h, chunk):
        ref = basis.at[h, x, pl.ds(chunk * 8, 8)]
        return remote(ref, ref, sy.at[chunk], ry.at[chunk], dy=4)

    def partner_rows(d, chunk, block_x):
        ref = basis.at[other, block_x, pl.ds(chunk * 8, 8)]
        return remote(ref, ref, sp.at[d, chunk], rp.at[d, chunk], dx=step[d])

    def partner_forward(d, i, block_x):
        ref = basis.at[other, block_x, pl.ds((d * 2 + i) * 8, 8)]
        return remote(ref, ref, spf.at[d, i], rpf.at[d, i], dx=step[d])

    before = (lax.rem(x + XS - 1, XS), lax.rem(x + 1, XS))
    far = lax.rem(x + 2, XS)

    loads[0].wait()
    for chunk in range(CHUNKS):
        go(across(mine, chunk))
    for d in range(2):
        go(own_rows(d, d, x))
    for d in range(2):
        go(own_rows(d, 1 - d, x))

    loads[1].wait()
    for t in range(4):
        diag[pl.ds(t * 64, 64), pl.ds(t * 64, 64)] = a_v[...]
    spreader = diag[...]
    dhi[...], dlo[...] = halves(spreader)
    thi[...], tlo[...] = halves(spreader.T)
    loads[2].wait()

    def reduce_samples(j, carry):
        m = pl.ds(pl.multiple_of(j * TILE, TILE), TILE)
        high, low = halves(x_v[:, :, m].reshape(256, TILE))
        y_part = nn(thi[...], high) + nn(thi[...], low) + nn(tlo[...], high)
        yhi[:, m], ylo[:, m] = halves(y_part)
        return carry

    lax.fori_loop(0, 2048 // TILE, reduce_samples, 0)

    for d in range(2):
        own_rows(d, d, before[d]).wait_recv()
        go(own_forward(d, before[d]))

    def send_partner(chunk):
        across(other, chunk).wait_recv()
        for d in range(2):
            go(partner_rows(d, chunk, x))

    def contract(h):
        def body(j, total):
            m = pl.ds(pl.multiple_of(j * 512, 512), 512)
            high, low = halves(basis[h, :, :, m].reshape(128, 512))
            bhi[h, :, m] = high
            blo[h, :, m] = low
            return total + nt(high, yhi[:, m]) + nt(high, ylo[:, m]) + nt(low, yhi[:, m])

        total = lax.fori_loop(0, 4, body, jnp.zeros((128, 256), f32))
        part[h] = total.reshape(XS, CORES, 16, 256)

    def scatter(h, i):
        dx, dc = NEAR[i]
        src = part.at[h, lax.rem(x + dx, XS), lax.rem(c + dc, CORES)]
        return remote(src, rs_in.at[h, i], s_rs.at[h, i], r_rs.at[h, i], dx=dx, dc=dc)

    def along_z(h, i):
        return remote(rs_sum.at[h], z_in.at[h, i], s_z.at[h, i], r_z.at[h, i], dz=i + 1)

    def along_y(h, i):
        return remote(z_sum.at[h], y_in.at[h, i], s_y.at[h, i], r_y.at[h, i], dy=i + 1)

    def start_scatter(h):
        for i in range(7):
            go(scatter(h, i))

    def scatter_to_z(h):
        for i in range(7):
            scatter(h, i).wait_recv()
        rs_sum[h] = part[h, x, c] + jnp.sum(rs_in[h], axis=0)
        for i in range(7):
            go(along_z(h, i))

    def z_to_y(h):
        for i in range(7):
            along_z(h, i).wait_recv()
        z_sum[h] = rs_sum[h] + jnp.sum(z_in[h], axis=0)
        for i in range(7):
            go(along_y(h, i))

    send_partner(0)
    send_partner(1)
    for d in range(2):
        own_rows(d, 1 - d, before[d]).wait_recv()
        own_forward(d, far).wait_recv()
    contract(mine)
    start_scatter(mine)
    send_partner(2)
    scatter_to_z(mine)
    send_partner(3)
    for i in range(2):
        for d in range(2):
            partner_rows(d, d * 2 + i, before[d]).wait_recv()
            go(partner_forward(d, i, before[d]))
    z_to_y(mine)
    for i in range(2):
        for d in range(2):
            partner_rows(d, (1 - d) * 2 + i, before[d]).wait_recv()
            partner_forward(d, i, far).wait_recv()
    contract(other)
    start_scatter(other)
    scatter_to_z(other)
    z_to_y(other)

    for h in range(2):
        for i in range(7):
            along_y(h, i).wait_recv()
        core[h, x, c] = z_sum[h] + jnp.sum(y_in[h], axis=0)

    def gather(i):
        dx, dc = NEAR[i]
        ref = core.at[:, x, c]
        return remote(ref, ref, s_ag.at[i], r_ag.at[i], dx=dx, dc=dc)

    for i in range(7):
        go(gather(i))
    for i in range(7):
        gather(i).wait_recv()

    chi, clo = halves(core[...].reshape(256, 256))
    spread = nt(dhi[...], chi) + nt(dhi[...], clo) + nt(dlo[...], chi)
    shi[...], slo[...] = halves(spread)

    for j in range(2048 // TILE):
        m = pl.ds(j * TILE, TILE)
        high, low = bhi[:, :, m].reshape(256, TILE), blo[:, :, m].reshape(256, TILE)
        removed = nn(shi[...], high) + nn(shi[...], low) + nn(slo[...], high)
        out_v[:, :, m] = x_v[:, :, m] - removed.reshape(4, 64, TILE)
    for copy in started:
        copy.wait_send()


def shards(snapshots, space_basis, sample_basis):
    vmem = pltpu.VMEM
    dma = pltpu.SemaphoreType.DMA
    hbm = pl.BlockSpec(memory_space=pltpu.HBM)
    return pl.pallas_call(
        kernel,
        name="deflate",
        out_shape=jax.ShapeDtypeStruct((4, 64, 2048), f32),
        in_specs=[hbm] * 3,
        out_specs=pl.BlockSpec(memory_space=pltpu.VMEM),
        scratch_shapes=[
            vmem((4, 64, 2048), f32),
            vmem((64, 64), f32),
            vmem((2, XS, 32, 2048), f32),
            vmem((2, 128, 2048), bf16),
            vmem((2, 128, 2048), bf16),
            vmem((256, 2048), bf16),
            vmem((256, 2048), bf16),
            vmem((256, 256), f32),
            vmem((256, 256), bf16),
            vmem((256, 256), bf16),
            vmem((256, 256), bf16),
            vmem((256, 256), bf16),
            vmem((2, XS, CORES, 16, 256), f32),
            vmem((2, 7, 16, 256), f32),
            vmem((2, 16, 256), f32),
            vmem((2, 7, 16, 256), f32),
            vmem((2, 16, 256), f32),
            vmem((2, 7, 16, 256), f32),
            vmem((2, XS, CORES, 16, 256), f32),
            vmem((256, 256), bf16),
            vmem((256, 256), bf16),
            dma((3,)),
            dma((CHUNKS,)), dma((CHUNKS,)),
            dma((2, 2)), dma((2, 2)),
            dma((2,)), dma((2,)),
            dma((2, CHUNKS)), dma((2, CHUNKS)),
            dma((2, 2)), dma((2, 2)),
            dma((2, 7)), dma((2, 7)),
            dma((2, 7)), dma((2, 7)),
            dma((2, 7)), dma((2, 7)),
            dma((7,)), dma((7,)),
        ],
        compiler_params=pltpu.CompilerParams(
            collective_id=0, has_side_effects=True, vmem_limit_bytes=32 * 2**20
        ),
    )(*(pltpu.with_memory_space_constraint(a, pltpu.HBM) for a in (snapshots, space_basis, sample_basis)))


def solution(mesh):
    return jax.shard_map(
        shards,
        mesh=mesh,
        in_specs=(P(None, "samp", "space"), P("samp", "space"), P("samp", None)),
        out_specs=P(None, "samp", "space"),
        check_vma=False,
    )
```

time: 131 us -> 65.8 us (0.50)
  blocking collectives: 117 us -> 0 us
  Pallas kernels: 0 us -> 64.3 us
  matrix products: 10.8 us -> 0 us
  local copies, waits for them, and re-layouts: 3.5 us -> 1.32 us
    all_to_all x4 -> x0, blocking collectives: 117 us -> none  [the longest x3 81.8 us: copy_for_each(): return lax.all_to_all(copies, axis, split_axis=0, concat_axis=0, tiled=True)]
    pallas_call x0 -> x1, Pallas kernels: none -> 64.3 us  [shards(): pl.pallas_call(kernel, name='deflate', out_shape=jax.ShapeDtypeStruct((4,...]
    dot_general x4 -> x0, matrix products: 10.8 us -> none  [the longest x1 5.11 us: shards(): lax.dot_general(full_basis, flattened, (((1,), (1,)), ((), ())), precisio...]
    dot_general x2 -> x0, local copies, waits for them, and re-layouts: 1.79 us -> none  [shards(): lax.dot_general(full_basis, flattened, (((1,), (1,)), ((), ())), precisio...]
    unnamed x2 -> x1, local copies, waits for them, and re-layouts: 0.01 us -> 1.32 us
where the time goes in v1:
time: 65.8 us; the launch traced here: 65.6 us
  Pallas kernels  64.3 us (98%)
  local copies, waits for them, and re-layouts  1.32 us (2%)
    pallas_call x1, Pallas kernels, shards(): pl.pallas_call(kernel, name='deflate', out_shape=jax.ShapeDtypeStruct((4,...  64.3 us
    unnamed x1, local copies, waits for them, and re-layouts  1.32 us

profile of v1, /device:TPU:1, one launch (start us, length us, event | category | flops | bytes accessed | tf_op | source)
XLA Modules:
  0.0 65.6 jit_solution(53777149412279543)
XLA Ops:
  0.0 64.3 %deflate.1 = f32[4,64,2048]{2,1,0:T(8,128)S(1)} custom-call(f32[4,64,2048]{2,1,0:T(8,128)} %x_hbm.1, f32[32,2048]{1,0:T(8,128)} %b_hbm.1, f32[64,64]{1,0:T(8,128)} %a_hbm.1), custom_call_target="tpu_custom_call" | custom-call | tf_op jit(solution)/shard_map/deflate/pallas_call | solution.py:249
  64.3 1.3 %copy.5 = f32[4,64,2048]{2,1,0:T(8,128)} copy(f32[4,64,2048]{2,1,0:T(8,128)S(1)} %deflate.1) | data formatting | bytes 4194304

commit v2 on v1

v2 whole, which is shorter than its diff:
```python
import jax
import jax.numpy as jnp
from jax import lax
from jax.experimental import pallas as pl
from jax.experimental.pallas import tpu as pltpu
from jax.sharding import PartitionSpec as P

MESH = pl.DeviceIdType.MESH
f32, bf16 = jnp.float32, jnp.bfloat16
XS, YS, ZS, CORES = 4, 8, 8, 2
CHUNKS = 4
FORWARDED = 4
SPLIT = 3
WINDOW = 3
TILE = 256


def position():
    space, samp = lax.axis_index("space"), lax.axis_index("samp")
    core, z = lax.rem(space, 2), lax.rem(lax.div(space, 2), ZS)
    y_lo, y_hi = lax.div(space, 2 * ZS), lax.rem(samp, 2)
    return lax.div(samp, 2), y_hi * 4 + y_lo, z, core


def device(at, dx=0, dy=0, dz=0, dc=0):
    x, y, z, core = at
    where = {}
    if isinstance(dy, int) and dy == 0:
        space, samp = lax.axis_index("space"), lax.axis_index("samp")
    else:
        y_new = lax.rem(y + dy, YS)
        space = (lax.rem(y_new, 4) * ZS + z) * 2 + core
        samp = x * 2 + lax.div(y_new, 4)
        where = {"space": space, "samp": samp}
    if not (isinstance(dx, int) and dx == 0):
        where["samp"] = samp + (lax.rem(x + dx, XS) - x) * 2
    if not (isinstance(dz, int) and dz == 0):
        space = space + (lax.rem(z + dz, ZS) - z) * 2
        where["space"] = space
    if dc:
        where["space"] = space + 1 - core * 2
    return where


NEAR = [(dx, dc) for dx in range(XS) for dc in range(CORES) if (dx, dc) != (0, 0)]


def halves(value):
    high = value.astype(bf16)
    return high, (value - high.astype(f32)).astype(bf16)


def nn(a, b):
    return jnp.dot(a, b, preferred_element_type=f32)


def nt(a, b):
    return lax.dot_general(a, b, (((1,), (1,)), ((), ())), preferred_element_type=f32)


def kernel(
    x_hbm, b_hbm, a_hbm, out_v,
    x_v, a_v, basis, bhi, blo, yhi, ylo, diag, dhi, dlo, thi, tlo,
    part, rs_in, rs_sum, z_in, z_sum, y_in, core, matrix, shi, slo,
    load_sem, sy, ry, sx, rx, sxf, rxf, sp, rp, s_rs, r_rs, s_z, r_z, s_y, r_y, s_ag, r_ag,
):
    at = position()
    x, y, z, c = at
    mine = lax.div(y, 4)
    other = 1 - mine

    loads = [
        pltpu.make_async_copy(
            b_hbm.at[pl.ds(i * 8, 8)], basis.at[mine, i, x], load_sem.at[i]
        )
        for i in range(CHUNKS)
    ]
    load_a = pltpu.make_async_copy(a_hbm, a_v, load_sem.at[CHUNKS])
    load_x = pltpu.make_async_copy(x_hbm, x_v, load_sem.at[CHUNKS + 1])
    for load in (*loads, load_a, load_x):
        load.start()

    barrier = pltpu.get_barrier_semaphore()
    partners = [dict(dy=d) for d in (4, 1, 7, 2, 6, 3, 5)]
    partners += [dict(dx=dx, dc=dc) for dx, dc in NEAR]
    partners += [dict(dz=d) for d in range(1, ZS)]
    for partner in partners:
        pl.semaphore_signal(
            barrier, inc=1, device_id=device(at, **partner), device_id_type=MESH
        )
    diag[...] = jnp.zeros_like(diag)
    for load in loads:
        load.wait()
    pl.semaphore_wait(barrier, len(partners))

    started = []

    def remote(src, dst, send, recv, **offset):
        return pltpu.make_async_remote_copy(
            src_ref=src,
            dst_ref=dst,
            send_sem=send,
            recv_sem=recv,
            device_id=device(at, **offset),
            device_id_type=MESH,
        )

    def go(copy):
        copy.start()
        started.append(copy)

    def drain(keep=0):
        while len(started) > keep:
            started.pop(0).wait_send()

    def across(h, i):
        ref = basis.at[h, i, x]
        return remote(ref, ref, sy.at[i], ry.at[i], dy=4)

    step = (1, XS - 1)
    before = (lax.rem(x + XS - 1, XS), lax.rem(x + 1, XS))
    far = lax.rem(x + 2, XS)

    def own_rows(d, half, block_x):
        ref = basis.at[mine, pl.ds(half * 2, 2), block_x]
        return remote(ref, ref, sx.at[d, half], rx.at[d, half], dx=step[d])

    def own_forward(d, block_x):
        ref = basis.at[mine, pl.ds(d * 2, 2), block_x]
        return remote(ref, ref, sxf.at[d], rxf.at[d], dx=step[d])

    def partner_rows(d, i, block_x):
        ref = basis.at[other, i, block_x]
        return remote(ref, ref, sp.at[i, d], rp.at[i, d], dx=step[d])

    def partner_far(i, block_x):
        ref = basis.at[other, i, block_x]
        dx = step[i % 2] if i < FORWARDED else 2
        return remote(ref, ref, sp.at[i, 2], rp.at[i, 2], dx=dx)

    for i in range(WINDOW):
        go(across(mine, i))
    for d in range(2):
        go(own_rows(d, d, x))
    for d in range(2):
        go(own_rows(d, 1 - d, x))

    load_a.wait()
    for t in range(4):
        diag[pl.ds(t * 64, 64), pl.ds(t * 64, 64)] = a_v[...]
    spreader = diag[...]
    dhi[...], dlo[...] = halves(spreader)
    thi[...], tlo[...] = halves(spreader.T)
    load_x.wait()

    def reduce_samples(j, carry):
        m = pl.ds(pl.multiple_of(j * TILE, TILE), TILE)
        high, low = halves(x_v[:, :, m].reshape(256, TILE))
        y_part = nn(thi[...], high) + nn(thi[...], low) + nn(tlo[...], high)
        yhi[:, m], ylo[:, m] = halves(y_part)
        return carry

    lax.fori_loop(0, 2048 // TILE, reduce_samples, 0)

    def send_partner(i):
        across(other, i).wait_recv()
        for d in range(2):
            go(partner_rows(d, i, x))
        if i >= FORWARDED:
            go(partner_far(i, x))
        if i + WINDOW < CHUNKS:
            go(across(mine, i + WINDOW))

    def contract(h, first, count):
        rows = count * 32

        def body(j, total):
            m = pl.ds(pl.multiple_of(j * 512, 512), 512)
            chunks = pl.ds(first, count)
            high, low = halves(basis[h, chunks, :, :, m].reshape(rows, 512))
            bhi[h, pl.ds(first * 32, rows), m] = high
            blo[h, pl.ds(first * 32, rows), m] = low
            return total + nt(high, yhi[:, m]) + nt(high, ylo[:, m]) + nt(low, yhi[:, m])

        total = lax.fori_loop(0, 4, body, jnp.zeros((rows, 256), f32))
        for half in range(CORES):
            part[h, half, pl.ds(first, count)] = total[
                :, half * 128 : half * 128 + 128
            ].reshape(count, XS, 8, 128)

    def scatter(batch, i):
        h, first, count, b = batch
        dx, dc = NEAR[i]
        chunks = pl.ds(first, count)
        src = part.at[h, lax.rem(c + dc, CORES), chunks, lax.rem(x + dx, XS)]
        sems = s_rs.at[h, b, i], r_rs.at[h, b, i]
        return remote(src, rs_in.at[h, i, chunks], *sems, dx=dx, dc=dc)

    def along_z(batch, i):
        h, first, count, b = batch
        chunks = pl.ds(first, count)
        sems = s_z.at[h, b, i], r_z.at[h, b, i]
        return remote(rs_sum.at[h, chunks], z_in.at[h, i, chunks], *sems, dz=i + 1)

    def along_y(batch, i):
        h, first, count, b = batch
        chunks = pl.ds(first, count)
        sems = s_y.at[h, b, i], r_y.at[h, b, i]
        return remote(z_sum.at[h, chunks], y_in.at[h, i, chunks], *sems, dy=i + 1)

    def start_scatter(batch):
        for i in range(7):
            go(scatter(batch, i))

    def scatter_to_z(batch):
        h, first, count, _ = batch
        chunks = pl.ds(first, count)
        for i in range(7):
            scatter(batch, i).wait_recv()
        rs_sum[h, chunks] = part[h, c, chunks, x] + jnp.sum(rs_in[h, :, chunks], axis=0)
        for i in range(7):
            go(along_z(batch, i))

    def z_to_y(batch):
        h, first, count, _ = batch
        chunks = pl.ds(first, count)
        for i in range(7):
            along_z(batch, i).wait_recv()
        z_sum[h, chunks] = rs_sum[h, chunks] + jnp.sum(z_in[h, :, chunks], axis=0)
        for i in range(7):
            go(along_y(batch, i))

    def pass_on(i):
        if i < FORWARDED:
            partner_rows(i % 2, i, before[i % 2]).wait_recv()
            go(partner_far(i, before[i % 2]))

    def arrived(i):
        for d in range(2):
            if i >= FORWARDED or d != i % 2:
                partner_rows(d, i, before[d]).wait_recv()
        partner_far(i, far).wait_recv()

    early = (mine, 0, CHUNKS, 0)
    late = [(other, 0, SPLIT, 0), (other, SPLIT, CHUNKS - SPLIT, 1)]

    for d in range(2):
        own_rows(d, d, before[d]).wait_recv()
        go(own_forward(d, before[d]))
    send_partner(0)
    for d in range(2):
        own_rows(d, 1 - d, before[d]).wait_recv()
        own_forward(d, far).wait_recv()
    contract(*early[:3])
    start_scatter(early)
    send_partner(1)
    pass_on(0)
    send_partner(2)
    pass_on(1)
    scatter_to_z(early)
    send_partner(3)
    pass_on(2)
    pass_on(3)
    z_to_y(early)
    arrived(0)
    arrived(1)
    arrived(2)
    contract(*late[0][:3])
    start_scatter(late[0])
    arrived(3)
    contract(*late[1][:3])
    start_scatter(late[1])
    scatter_to_z(late[0])
    scatter_to_z(late[1])
    drain(keep=28)
    z_to_y(late[0])
    z_to_y(late[1])
    drain(keep=14)

    for h in range(2):
        for i in range(7):
            source = lax.div(lax.rem(y + YS - 1 - i, YS), 4)
            pl.when(source == h)(along_y((h, 0, CHUNKS, 0), i).wait_recv)

            @pl.when(source != h)
            def _():
                along_y((h, 0, SPLIT, 0), i).wait_recv()
                along_y((h, SPLIT, CHUNKS - SPLIT, 1), i).wait_recv()

        core[x, c, h] = z_sum[h] + jnp.sum(y_in[h], axis=0)

    def gather(i):
        dx, dc = NEAR[i]
        ref = core.at[x, c]
        return remote(ref, ref, s_ag.at[i], r_ag.at[i], dx=dx, dc=dc)

    for i in range(7):
        go(gather(i))
    drain(keep=7)
    for i in range(7):
        gather(i).wait_recv()

    for h in range(2):
        for i in range(CHUNKS):
            for block in range(XS):
                for half in range(CORES):
                    rows = pl.ds(((h * CHUNKS + i) * XS + block) * 8, 8)
                    matrix[rows, pl.ds(half * 128, 128)] = core[block, half, h, i]
    chi, clo = halves(matrix[...])
    spread = nt(dhi[...], chi) + nt(dhi[...], clo) + nt(dlo[...], chi)
    shi[...], slo[...] = halves(spread)

    for j in range(2048 // TILE):
        m = pl.ds(j * TILE, TILE)
        high, low = bhi[:, :, m].reshape(256, TILE), blo[:, :, m].reshape(256, TILE)
        removed = nn(shi[...], high) + nn(shi[...], low) + nn(slo[...], high)
        out_v[:, :, m] = x_v[:, :, m] - removed.reshape(4, 64, TILE)
    drain()


def shards(snapshots, space_basis, sample_basis):
    vmem = pltpu.VMEM
    dma = pltpu.SemaphoreType.DMA
    hbm = pl.BlockSpec(memory_space=pltpu.HBM)
    return pl.pallas_call(
        kernel,
        name="deflate",
        out_shape=jax.ShapeDtypeStruct((4, 64, 2048), f32),
        in_specs=[hbm] * 3,
        out_specs=pl.BlockSpec(memory_space=pltpu.VMEM),
        scratch_shapes=[
            vmem((4, 64, 2048), f32),
            vmem((64, 64), f32),
            vmem((2, CHUNKS, XS, 8, 2048), f32),
            vmem((2, 128, 2048), bf16),
            vmem((2, 128, 2048), bf16),
            vmem((256, 2048), bf16),
            vmem((256, 2048), bf16),
            vmem((256, 256), f32),
            vmem((256, 256), bf16),
            vmem((256, 256), bf16),
            vmem((256, 256), bf16),
            vmem((256, 256), bf16),
            vmem((2, CORES, CHUNKS, XS, 8, 128), f32),
            vmem((2, 7, CHUNKS, 8, 128), f32),
            vmem((2, CHUNKS, 8, 128), f32),
            vmem((2, 7, CHUNKS, 8, 128), f32),
            vmem((2, CHUNKS, 8, 128), f32),
            vmem((2, 7, CHUNKS, 8, 128), f32),
            vmem((XS, CORES, 2, CHUNKS, 8, 128), f32),
            vmem((256, 256), f32),
            vmem((256, 256), bf16),
            vmem((256, 256), bf16),
            dma((CHUNKS + 2,)),
            dma((CHUNKS,)), dma((CHUNKS,)),
            dma((2, 2)), dma((2, 2)),
            dma((2,)), dma((2,)),
            dma((CHUNKS, 3)), dma((CHUNKS, 3)),
            dma((2, 2, 7)), dma((2, 2, 7)),
            dma((2, 2, 7)), dma((2, 2, 7)),
            dma((2, 2, 7)), dma((2, 2, 7)),
            dma((7,)), dma((7,)),
        ],
        compiler_params=pltpu.CompilerParams(
            collective_id=0, has_side_effects=True, vmem_limit_bytes=32 * 2**20
        ),
    )(*(pltpu.with_memory_space_constraint(a, pltpu.HBM) for a in (snapshots, space_basis, sample_basis)))


def solution(mesh):
    return jax.shard_map(
        shards,
        mesh=mesh,
        in_specs=(P(None, "samp", "space"), P("samp", "space"), P("samp", None)),
        out_specs=P(None, "samp", "space"),
        check_vma=False,
    )
```

time: 65.8 us -> 65 us (0.988)
  Pallas kernels: 64.3 us -> 63.5 us
    pallas_call x1, Pallas kernels: 64.3 us -> 63.5 us  [shards(): pl.pallas_call(kernel, name='deflate', out_shape=jax.ShapeDtypeStruct((4,...]
where the time goes in v2:
time: 65 us; the launch traced here: 64.9 us
  Pallas kernels  63.5 us (98%)
  local copies, waits for them, and re-layouts  1.32 us (2%)
    pallas_call x1, Pallas kernels, shards(): pl.pallas_call(kernel, name='deflate', out_shape=jax.ShapeDtypeStruct((4,...  63.5 us
    unnamed x1, local copies, waits for them, and re-layouts  1.32 us

profile of v2, /device:TPU:1, one launch (start us, length us, event | category | flops | bytes accessed | tf_op | source)
XLA Modules:
  0.0 64.9 jit_solution(7037107225741461922)
XLA Ops:
  0.0 63.5 %deflate.1 = f32[4,64,2048]{2,1,0:T(8,128)S(1)} custom-call(f32[4,64,2048]{2,1,0:T(8,128)} %x_hbm.1, f32[32,2048]{1,0:T(8,128)} %b_hbm.1, f32[64,64]{1,0:T(8,128)} %a_hbm.1), custom_call_target="tpu_custom_call" | custom-call | tf_op jit(solution)/shard_map/deflate/pallas_call | solution.py:325
  63.5 1.3 %copy.5 = f32[4,64,2048]{2,1,0:T(8,128)} copy(f32[4,64,2048]{2,1,0:T(8,128)S(1)} %deflate.1) | data formatting | bytes 4194304

commit v3 on v2

--- a/solution.py
+++ b/solution.py
@@ -9,8 +9,8 @@
 f32, bf16 = jnp.float32, jnp.bfloat16
 XS, YS, ZS, CORES = 4, 8, 8, 2
 CHUNKS = 4
-FORWARDED = 4
-SPLIT = 3
+FORWARDED = 2
+SPLIT = 2
 WINDOW = 3
 TILE = 256
 
@@ -44,6 +44,9 @@
 
 NEAR = [(dx, dc) for dx in range(XS) for dc in range(CORES) if (dx, dc) != (0, 0)]
 
+NEAR_ORDER = (4, 3, 2, 6, 1, 5, 0)
+FAR_FIRST = (3, 2, 4, 1, 5, 0, 6)
+
 
 def halves(value):
     high = value.astype(bf16)
@@ -61,7 +64,7 @@
 def kernel(
     x_hbm, b_hbm, a_hbm, out_v,
     x_v, a_v, basis, bhi, blo, yhi, ylo, diag, dhi, dlo, thi, tlo,
-    part, rs_in, rs_sum, z_in, z_sum, y_in, core, matrix, shi, slo,
+    part, rs_in, rs_sum, z_in, z_sum, y_in, core, matrix, spread,
     load_sem, sy, ry, sx, rx, sxf, rxf, sp, rp, s_rs, r_rs, s_z, r_z, s_y, r_y, s_ag, r_ag,
 ):
     at = position()
@@ -178,8 +181,9 @@
             m = pl.ds(pl.multiple_of(j * 512, 512), 512)
             chunks = pl.ds(first, count)
             high, low = halves(basis[h, chunks, :, :, m].reshape(rows, 512))
-            bhi[h, pl.ds(first * 32, rows), m] = high
-            blo[h, pl.ds(first * 32, rows), m] = low
+            parts = pl.ds(first // SPLIT, count // SPLIT)
+            bhi[parts, h, :, m] = high.reshape(count // SPLIT, SPLIT * 32, 512)
+            blo[parts, h, :, m] = low.reshape(count // SPLIT, SPLIT * 32, 512)
             return total + nt(high, yhi[:, m]) + nt(high, ylo[:, m]) + nt(low, yhi[:, m])
 
         total = lax.fori_loop(0, 4, body, jnp.zeros((rows, 256), f32))
@@ -209,7 +213,7 @@
         return remote(z_sum.at[h, chunks], y_in.at[h, i, chunks], *sems, dy=i + 1)
 
     def start_scatter(batch):
-        for i in range(7):
+        for i in NEAR_ORDER:
             go(scatter(batch, i))
 
     def scatter_to_z(batch):
@@ -218,7 +222,7 @@
         for i in range(7):
             scatter(batch, i).wait_recv()
         rs_sum[h, chunks] = part[h, c, chunks, x] + jnp.sum(rs_in[h, :, chunks], axis=0)
-        for i in range(7):
+        for i in FAR_FIRST:
             go(along_z(batch, i))
 
     def z_to_y(batch):
@@ -227,7 +231,7 @@
         for i in range(7):
             along_z(batch, i).wait_recv()
         z_sum[h, chunks] = rs_sum[h, chunks] + jnp.sum(z_in[h, :, chunks], axis=0)
-        for i in range(7):
+        for i in FAR_FIRST:
             go(along_y(batch, i))
 
     def pass_on(i):
@@ -264,9 +268,9 @@
     z_to_y(early)
     arrived(0)
     arrived(1)
-    arrived(2)
     contract(*late[0][:3])
     start_scatter(late[0])
+    arrived(2)
     arrived(3)
     contract(*late[1][:3])
     start_scatter(late[1])
@@ -277,44 +281,47 @@
     z_to_y(late[1])
     drain(keep=14)
 
-    for h in range(2):
+    def sum_over_y(b):
+        chunks = pl.ds(b * SPLIT, SPLIT)
+        for h in range(2):
+            for i in range(7):
+                source = lax.div(lax.rem(y + YS - 1 - i, YS), 4)
+                if b == 0:
+                    pl.when(source == h)(along_y((h, 0, CHUNKS, 0), i).wait_recv)
+                pl.when(source != h)(along_y((h, b * SPLIT, SPLIT, b), i).wait_recv)
+            core[x, c, h, chunks] = z_sum[h, chunks] + jnp.sum(y_in[h, :, chunks], axis=0)
+
+    def gather(b, i):
+        dx, dc = NEAR[i]
+        ref = core.at[x, c, :, pl.ds(b * SPLIT, SPLIT)]
+        return remote(ref, ref, s_ag.at[b, i], r_ag.at[b, i], dx=dx, dc=dc)
+
+    for b in range(2):
+        sum_over_y(b)
+        for i in NEAR_ORDER:
+            go(gather(b, i))
+    drain(keep=14)
+
+    for b in range(2):
         for i in range(7):
-            source = lax.div(lax.rem(y + YS - 1 - i, YS), 4)
-            pl.when(source == h)(along_y((h, 0, CHUNKS, 0), i).wait_recv)
-
-            @pl.when(source != h)
-            def _():
-                along_y((h, 0, SPLIT, 0), i).wait_recv()
-                along_y((h, SPLIT, CHUNKS - SPLIT, 1), i).wait_recv()
-
-        core[x, c, h] = z_sum[h] + jnp.sum(y_in[h], axis=0)
-
-    def gather(i):
-        dx, dc = NEAR[i]
-        ref = core.at[x, c]
-        return remote(ref, ref, s_ag.at[i], r_ag.at[i], dx=dx, dc=dc)
-
-    for i in range(7):
-        go(gather(i))
-    drain(keep=7)
-    for i in range(7):
-        gather(i).wait_recv()
-
-    for h in range(2):
-        for i in range(CHUNKS):
-            for block in range(XS):
-                for half in range(CORES):
-                    rows = pl.ds(((h * CHUNKS + i) * XS + block) * 8, 8)
-                    matrix[rows, pl.ds(half * 128, 128)] = core[block, half, h, i]
-    chi, clo = halves(matrix[...])
-    spread = nt(dhi[...], chi) + nt(dhi[...], clo) + nt(dlo[...], chi)
-    shi[...], slo[...] = halves(spread)
-
-    for j in range(2048 // TILE):
-        m = pl.ds(j * TILE, TILE)
-        high, low = bhi[:, :, m].reshape(256, TILE), blo[:, :, m].reshape(256, TILE)
-        removed = nn(shi[...], high) + nn(shi[...], low) + nn(slo[...], high)
-        out_v[:, :, m] = x_v[:, :, m] - removed.reshape(4, 64, TILE)
+            gather(b, i).wait_recv()
+        for h in range(2):
+            for i in range(SPLIT):
+                for block in range(XS):
+                    for half in range(CORES):
+                        rows = pl.ds(((h * SPLIT + i) * XS + block) * 8, 8)
+                        matrix[rows, pl.ds(half * 128, 128)] = core[
+                            block, half, h, b * SPLIT + i
+                        ]
+        chi, clo = halves(matrix[...])
+        high, low = halves(nt(dhi[...], chi) + nt(dhi[...], clo) + nt(dlo[...], chi))
+        spread[...] = jnp.concatenate([high, low, high], axis=1)
+        for j in range(2048 // TILE):
+            m = pl.ds(j * TILE, TILE)
+            high, low = bhi[b, :, :, m].reshape(128, TILE), blo[b, :, :, m].reshape(128, TILE)
+            removed = nn(spread[...], jnp.concatenate([high, high, low], axis=0))
+            kept = x_v if b == 0 else out_v
+            out_v[:, :, m] = kept[:, :, m] - removed.reshape(4, 64, TILE)
     drain()
 
 
@@ -332,8 +339,8 @@
             vmem((4, 64, 2048), f32),
             vmem((64, 64), f32),
             vmem((2, CHUNKS, XS, 8, 2048), f32),
-            vmem((2, 128, 2048), bf16),
-            vmem((2, 128, 2048), bf16),
+            vmem((2, 2, SPLIT * 32, 2048), bf16),
+            vmem((2, 2, SPLIT * 32, 2048), bf16),
             vmem((256, 2048), bf16),
             vmem((256, 2048), bf16),
             vmem((256, 256), f32),
@@ -348,9 +355,8 @@
             vmem((2, CHUNKS, 8, 128), f32),
             vmem((2, 7, CHUNKS, 8, 128), f32),
             vmem((XS, CORES, 2, CHUNKS, 8, 128), f32),
-            vmem((256, 256), f32),
-            vmem((256, 256), bf16),
-            vmem((256, 256), bf16),
+            vmem((128, 256), f32),
+            vmem((256, 384), bf16),
             dma((CHUNKS + 2,)),
             dma((CHUNKS,)), dma((CHUNKS,)),
             dma((2, 2)), dma((2, 2)),
@@ -359,7 +365,7 @@
             dma((2, 2, 7)), dma((2, 2, 7)),
             dma((2, 2, 7)), dma((2, 2, 7)),
             dma((2, 2, 7)), dma((2, 2, 7)),
-            dma((7,)), dma((7,)),
+            dma((2, 7)), dma((2, 7)),
         ],
         compiler_params=pltpu.CompilerParams(
             collective_id=0, has_side_effects=True, vmem_limit_bytes=32 * 2**20

time: 65 us -> 62.7 us (0.965)
  Pallas kernels: 63.5 us -> 61.3 us
    pallas_call x1, Pallas kernels: 63.5 us -> 61.3 us  [shards(): pl.pallas_call(kernel, name='deflate', out_shape=jax.ShapeDtypeStruct((4,...]
where the time goes in v3:
time: 62.7 us; the launch traced here: 62.6 us
  Pallas kernels  61.3 us (98%)
  local copies, waits for them, and re-layouts  1.32 us (2%)
    pallas_call x1, Pallas kernels, shards(): pl.pallas_call(kernel, name='deflate', out_shape=jax.ShapeDtypeStruct((4,...  61.3 us
    unnamed x1, local copies, waits for them, and re-layouts  1.32 us

profile of v3, /device:TPU:1, one launch (start us, length us, event | category | flops | bytes accessed | tf_op | source)
XLA Modules:
  0.0 62.6 jit_solution(14752513733141517641)
XLA Ops:
  0.0 61.3 %deflate.1 = f32[4,64,2048]{2,1,0:T(8,128)S(1)} custom-call(f32[4,64,2048]{2,1,0:T(8,128)} %x_hbm.1, f32[32,2048]{1,0:T(8,128)} %b_hbm.1, f32[64,64]{1,0:T(8,128)} %a_hbm.1), custom_call_target="tpu_custom_call" | custom-call | tf_op jit(solution)/shard_map/deflate/pallas_call | solution.py:332
  61.3 1.3 %copy.5 = f32[4,64,2048]{2,1,0:T(8,128)} copy(f32[4,64,2048]{2,1,0:T(8,128)S(1)} %deflate.1) | data formatting | bytes 4194304

commit v4 on v3

--- a/solution.py
+++ b/solution.py
@@ -128,9 +128,9 @@
         ref = basis.at[mine, pl.ds(half * 2, 2), block_x]
         return remote(ref, ref, sx.at[d, half], rx.at[d, half], dx=step[d])
 
-    def own_forward(d, block_x):
-        ref = basis.at[mine, pl.ds(d * 2, 2), block_x]
-        return remote(ref, ref, sxf.at[d], rxf.at[d], dx=step[d])
+    def own_far(half, block_x):
+        ref = basis.at[mine, pl.ds(half * 2, 2), block_x]
+        return remote(ref, ref, sxf.at[half], rxf.at[half], dx=2)
 
     def partner_rows(d, i, block_x):
         ref = basis.at[other, i, block_x]
@@ -145,6 +145,8 @@
         go(across(mine, i))
     for d in range(2):
         go(own_rows(d, d, x))
+    for half in range(2):
+        go(own_far(half, x))
     for d in range(2):
         go(own_rows(d, 1 - d, x))
 
@@ -248,13 +250,11 @@
     early = (mine, 0, CHUNKS, 0)
     late = [(other, 0, SPLIT, 0), (other, SPLIT, CHUNKS - SPLIT, 1)]
 
+    send_partner(0)
     for d in range(2):
         own_rows(d, d, before[d]).wait_recv()
-        go(own_forward(d, before[d]))
-    send_partner(0)
-    for d in range(2):
         own_rows(d, 1 - d, before[d]).wait_recv()
-        own_forward(d, far).wait_recv()
+        own_far(d, far).wait_recv()
     contract(*early[:3])
     start_scatter(early)
     send_partner(1)

time: 62.7 us -> 65.8 us (1.049)
  Pallas kernels: 61.3 us -> 64.4 us
    pallas_call x1, Pallas kernels: 61.3 us -> 64.4 us  [shards(): pl.pallas_call(kernel, name='deflate', out_shape=jax.ShapeDtypeStruct((4,...]
where the time goes in v4:
time: 65.8 us; the launch traced here: 65.7 us
  Pallas kernels  64.4 us (98%)
  local copies, waits for them, and re-layouts  1.32 us (2%)
    pallas_call x1, Pallas kernels, shards(): pl.pallas_call(kernel, name='deflate', out_shape=jax.ShapeDtypeStruct((4,...  64.4 us
    unnamed x1, local copies, waits for them, and re-layouts  1.32 us

profile of v4, /device:TPU:1, one launch (start us, length us, event | category | flops | bytes accessed | tf_op | source)
XLA Modules:
  0.0 65.7 jit_solution(14410578919681072697)
XLA Ops:
  0.0 64.4 %deflate.1 = f32[4,64,2048]{2,1,0:T(8,128)S(1)} custom-call(f32[4,64,2048]{2,1,0:T(8,128)} %x_hbm.1, f32[32,2048]{1,0:T(8,128)} %b_hbm.1, f32[64,64]{1,0:T(8,128)} %a_hbm.1), custom_call_target="tpu_custom_call" | custom-call | tf_op jit(solution)/shard_map/deflate/pallas_call | solution.py:332
  64.4 1.3 %copy.5 = f32[4,64,2048]{2,1,0:T(8,128)} copy(f32[4,64,2048]{2,1,0:T(8,128)S(1)} %deflate.1) | data formatting | bytes 4194304
